TPU v7x, 32 devices: a whole 2x2x4 slice. The times are simulated.
32 devices in a mesh: section: 2 (over core), expert: 16 (over z, y, x).
Axes of the slice: x: 2, y: 2, z: 4, core: 2. Of those that a mesh axis runs over, the one named last changes fastest.
Arguments:
- inputs: bfloat16 [2, 2, 2048, 512], P('section', None, 'expert'), may hold values from -6 to 6
- cotangent: bfloat16 [2, 2, 2048, 512], P('section', None, 'expert'), may hold values from -6 to 6
- segments: int32 [2, 2, 2048], P('section', None, 'expert'), may hold values from 0 to 63, never falling along the last dimension, each value on 1 to 128 neighbouring positions
- tasks: int32 [2, 2, 2048, 1], P('section', None, 'expert'), may hold values from 0 to 7; in each aligned block of 128 rows (0 to 127, 128 to 255, ..., all dimensions but the last counted through in order) at most 48 rows name the same one
- table: int32 [2, 8, 2], P('section'), may hold values from 0 to 15, as said below
- capacity: int32 [2], P('section'), may hold values from 192 to 256, as said below
- gains: float32 [2, 3, 512], P('section'), may hold values from 0.1 to 1.9
- w_qkv: bfloat16 [2, 512, 1536], P('section'), may hold values from -0.25 to 0.25
- w_out: bfloat16 [2, 512, 512], P('section'), may hold values from -0.75 to 0.75
- w_cross: bfloat16 [2, 512, 1024], P('section')
- w_router: bfloat16 [2, 512, 16], P('section'), may hold values from -0.1875 to 0.1875
- w_up: bfloat16 [2, 16, 512, 2048], P('section', 'expert'), may hold values from -0.25 to 0.25
- w_down: bfloat16 [2, 16, 2048, 512], P('section', 'expert'), may hold values from -0.125 to 0.125
Outputs:
- layer_out: bfloat16 [2, 2, 2048, 512], P('section', None, 'expert')
- inputs_grad: float32 [2, 2, 2048, 512], P('section', None, 'expert')
- gains_grad: float32 [2, 3, 512], P('section')
- w_qkv_grad: float32 [2, 512, 1536], P('section')
- w_out_grad: float32 [2, 512, 512], P('section')
- w_cross_grad: float32 [2, 512, 1024], P('section')
- w_router_grad: float32 [2, 512, 16], P('section')
- w_up_grad: float32 [2, 16, 512, 2048], P('section', 'expert')
- w_down_grad: float32 [2, 16, 2048, 512], P('section', 'expert')
Inputs may be any that keep to these rules, and one draw needn't show every extreme that they name: `tasks`: in each device's rows of one micro-batch (aligned blocks of 128 tokens) no task occurs more than 48 times, and some task occurs exactly that often. `table`: for each layer every expert belongs to exactly one task, and a task's two experts differ. One of the two layers has capacity 256.
All inputs are finite; a program needn't handle non-finite values.
Results may differ from a plain program's by a relative error of at most 0.015.
Values may be sent and summed in bfloat16 or wider, within the bound.
A program may use at most 192 MiB of HBM per device.

v0:
```python
import math
from types import SimpleNamespace

import jax
import jax.numpy as jnp
from jax import lax
from jax.experimental import pallas as pl
from jax.experimental.pallas import tpu as pltpu
from jax.sharding import PartitionSpec as P

HEADS = 8
EPSILON = 1e-06
LANES = 128
UNROLL = 4
MESH = pl.DeviceIdType.MESH
F32 = jnp.float32
BF16 = jnp.bfloat16

INFO_TASK, INFO_RANK, INFO_COUNT = (0, 2, 4)
ROWS, REPLY, MIRROR, SUMS, MEMORY, SENT = (1000, 2000, 3000, 4000, 5000, 10000)


def round_up(value, unit):
    return -(-value // unit) * unit


def dot(left, right):
    return jnp.dot(left, right, preferred_element_type=F32)


def dot_rows(left, right):
    return lax.dot_general(left, right, (((0,), (0,)), ((), ())), preferred_element_type=F32)


def dot_cols(left, right):
    return lax.dot_general(left, right, (((1,), (1,)), ((), ())), preferred_element_type=F32)


def lane_sum(value):
    return jnp.sum(value, axis=-1, keepdims=True)


def row_sum(value):
    return jnp.sum(value, axis=0, keepdims=True)


def when_equal(left, right, value=1.0):
    return jnp.where(left == right, value, 0.0)


def iota(shape, axis):
    return lax.broadcasted_iota(jnp.int32, shape, axis).astype(F32)


def whole_part(value, unit):
    return jnp.floor((value + 0.5) * (1.0 / unit))


def inverse_rms(value):
    return lax.rsqrt(jnp.mean(value * value, axis=-1, keepdims=True) + EPSILON)


def norm(value, gain):
    return value * inverse_rms(value) * gain


def norm_back(value, gain, grad):
    scale = inverse_rms(value)
    unit = value * scale
    scaled = grad * gain
    grad_value = scale * (scaled - unit * jnp.mean(scaled * unit, axis=-1, keepdims=True))
    return grad_value, row_sum(grad * unit)


def gelu_and_slope(hidden):
    rate = math.sqrt(2.0 / math.pi)
    square = hidden * hidden
    bend = jnp.tanh(hidden * (rate + rate * 0.044715 * square))
    share = 0.5 + 0.5 * bend
    act = hidden * share
    slope = share + act * (1.0 - bend) * (rate + 3.0 * rate * 0.044715 * square)
    return act, slope


class Sizes:
    def __init__(self, inputs, w_qkv, w_cross, w_router, w_up, table, experts):
        _, self.micro, self.tok, self.model = inputs.shape
        self.hidden = w_up.shape[-1]
        self.experts = experts
        self.tasks = table.shape[1]
        self.slots = 2 * self.tok
        self.halves = 2
        self.group = experts // self.halves
        self.bound = max(2, 6 * self.tok // experts)
        self.send = round_up(self.bound, 16)
        self.merged = self.halves * self.bound <= self.send
        self.flights = 1 if self.merged else self.halves
        self.half_rows = self.group * self.send
        self.all_rows = self.flights * self.half_rows
        self.misc = round_up(w_router.shape[-1] + 3, LANES)
        self.qkv_blocks = w_qkv.shape[-1] // LANES
        self.out_blocks = self.model // LANES
        self.cross_blocks = w_cross.shape[-1] // LANES
        self.misc_blocks = self.misc // LANES
        self.blocks = self.qkv_blocks + self.out_blocks + self.cross_blocks + self.misc_blocks
        self.bits = experts.bit_length() - 1
        unit = 16 * experts
        self.groups = []
        start = 0
        for blocks, count in (
            (self.cross_blocks, 3),
            (self.out_blocks, 2),
            (self.qkv_blocks + self.misc_blocks, 6),
        ):
            units = -(-blocks * self.model // unit)
            count = min(count, units)
            group = []
            for part in range(count):
                size = (units // count + (part < units % count)) * unit
                group.append((start, size))
                start += size
            self.groups.append(group)
        self.parts = sum(len(group) for group in self.groups)
        self.dense_rows = start


def kernel_body(z, names, *refs):
    r = SimpleNamespace(**dict(zip(names, refs)))
    me = lax.axis_index("expert")
    section = lax.axis_index("section")
    tok, model, micro, group, send, slots = (z.tok, z.model, z.micro, z.group, z.send, z.slots)
    here = lax.rem(me, group)
    base = me - here
    mirror = lax.rem(me + group, z.experts)
    me_f = me.astype(F32)
    here_f = here.astype(F32)
    base_f = base.astype(F32)
    enc_f = 1.0 - section.astype(F32)

    side = [None]
    owed = {}

    def on_section(index):
        def put(run):
            side[0] = index
            pl.when(section == index)(run)
            side[0] = None

        return put

    enc, dec = (on_section(0), on_section(1))

    def wait_for(ref, sem):
        pltpu.make_async_copy(ref, ref, sem).wait()

    def owe(key, copy):
        owed[side[0], key] = copy

    def settle(key):
        found = [e for e in owed if e[1] == key and (side[0] in (None, e[0]) or e[0] is None)]
        copies = [owed.pop(entry) for entry in found]
        if side[0] is not None and found[0][0] is None:
            owed[1 - side[0], key] = copies[0]
        wait_for(*copies[0]())

    def settle_all():
        for index in (None, 0, 1):
            waits = [owed.pop(entry) for entry in list(owed) if entry[0] == index]

            def run():
                for copy in waits:
                    wait_for(*copy())

            if index is None:
                run()
            else:
                pl.when(section == index)(run)

    loads = [
        pltpu.make_async_copy(source, target, r.load_sem.at[i])
        for i, (source, target) in enumerate(
            (
                (r.w_qkv, r.wqkv),
                (r.w_out, r.wout),
                (r.w_cross, r.wcross),
                (r.w_up, r.wup),
                (r.w_down, r.wdown),
            )
        )
    ]
    for load in loads:
        load.start()

    barrier = pltpu.get_barrier_semaphore()

    def greet(step, _):
        pl.semaphore_signal(
            barrier,
            inc=1,
            device_id={"expert": lax.rem(me + step, z.experts)},
            device_id_type=MESH,
        )
        return 0

    lax.fori_loop(1, z.experts, greet, 0)
    pl.semaphore_signal(
        barrier, inc=1, device_id={"section": 1 - section}, device_id_type=MESH
    )

    seg_rows = r.segments[...].astype(F32)
    task_rows = r.tasks[...].astype(F32)
    blank = jnp.zeros((LANES - 2 * micro, LANES), F32)
    flipped = jnp.transpose(jnp.concatenate([seg_rows, task_rows, blank], axis=0))
    lane = iota((1, LANES), 1)
    earlier = jnp.where(iota((tok, tok), 0) < iota((tok, tok), 1), 1.0, 0.0)
    ranks, counts = ([], [])
    for m in range(micro):
        task_col = flipped[:, micro + m : micro + m + 1]
        ranks.append(row_sum(when_equal(task_col, task_rows[m : m + 1]) * earlier))
        counts.append(row_sum(when_equal(task_col, lane)))
    r.infos[0] = jnp.concatenate(
        [task_rows, *ranks, *counts, jnp.zeros((8 - 3 * micro, LANES), F32)], axis=0
    )

    table = r.table[...].astype(F32)
    table_lane = iota((1, z.tasks), 1)

    def task_of(expert):
        return lane_sum(
            when_equal(table[0:1], expert, table_lane) + when_equal(table[1:2], expert, table_lane)
        )

    line = iota((z.half_rows, 1), 0)
    line_block = whole_part(line, send)
    line_rank = line - line_block * send
    line_place = here_f + line_block
    line_place = jnp.where(line_place >= group, line_place - group, line_place)
    line_task = task_of(base_f + line_place)

    def fill_pick(half):
        rank_here = line_rank - (half * z.bound if z.merged else 0)
        info = r.infos[half * group]
        for m in range(micro):
            hit = (info[INFO_TASK + m : INFO_TASK + m + 1] == line_task) & (
                info[INFO_RANK + m : INFO_RANK + m + 1] == rank_here
            )
            r.pick[half, m] = jnp.where(hit, 1.0, 0.0).astype(BF16)

    fill_pick(0)

    def greet_back():
        pl.semaphore_wait(barrier, z.experts)

        def tell(step, _):
            pltpu.make_async_remote_copy(
                src_ref=r.infos.at[0],
                dst_ref=r.infos.at[step],
                send_sem=r.info_send,
                recv_sem=r.info_recv,
                device_id={"expert": lax.rem(me + step, z.experts)},
                device_id_type=MESH,
            ).start()
            return 0

        lax.fori_loop(1, z.experts, tell, 0)
        others_told = pl.ds(1, z.experts - 1)
        owe(SENT, lambda: (r.infos.at[others_told], r.info_send))
        owe(0, lambda: (r.infos.at[others_told], r.info_recv))

    def spread(way, m, half, rows, back):
        packed, landed = (
            (r.reply_out, r.reply_in) if back else (r.rows_out, r.rows_in)
        )
        send_sem, recv_sem = (
            (r.reply_send, r.reply_recv) if back else (r.rows_send, r.rows_recv)
        )
        packed[way, m, half] = rows.reshape(group, send, model)
        landed[way, m, half, 0] = rows[:send]

        def push(step, _):
            if back:
                other = lax.rem(here + group - step, group)
            else:
                other = lax.rem(here + step, group)
            pltpu.make_async_remote_copy(
                src_ref=packed.at[way, m, half, step],
                dst_ref=landed.at[way, m, half, step],
                send_sem=send_sem.at[way, m, half],
                recv_sem=recv_sem.at[way, m, half],
                device_id={"expert": base + other},
                device_id_type=MESH,
            ).start()
            return 0

        lax.fori_loop(1, group, push, 0, unroll=group <= 8)
        key = (REPLY if back else ROWS) + 100 * way + 10 * m + half
        others = pl.ds(1, group - 1)
        at = (way, m, half)
        owe(SENT + key, lambda: (packed.at[(*at, others)], send_sem.at[at]))
        owe(key, lambda: (landed.at[(*at, others)], recv_sem.at[at]))

    def ship(key, source, target, sems, device_id):
        copy = pltpu.make_async_remote_copy(
            src_ref=source(),
            dst_ref=target(),
            send_sem=sems()[0],
            recv_sem=sems()[1],
            device_id=device_id,
            device_id_type=MESH,
        )
        copy.start()
        owe(SENT + key, lambda: (source(), sems()[0]))

    def swap(key, source, target, sems):
        ship(key, source, target, sems, {"expert": mirror})
        owe(key, lambda: (target(), sems()[1]))

    def dispatch(way, m, source):
        swap(
            MIRROR + 10 * way + m,
            lambda: source.at[m],
            lambda: r.mirror_rows.at[way, m],
            lambda: (r.mirror_send.at[way, m], r.mirror_recv.at[way, m]),
        )
        if not z.merged:
            spread(way, m, 0, dot(r.pick[0, m], source[m]).astype(BF16), False)

    def dispatch_mirror(way, m, source):
        settle(MIRROR + 10 * way + m)
        rows = dot(r.pick[1, m], r.mirror_rows[way, m])
        if z.merged:
            rows += dot(r.pick[0, m], source[m])
        spread(way, m, z.flights - 1, rows.astype(BF16), False)

    def arrived(way, m):
        for half in range(z.flights):
            settle(ROWS + 100 * way + 10 * m + half)
        return dot(r.compact[m], r.rows_in[way, m].reshape(z.all_rows, model))

    def combine(way, m, rows):
        reply = dot_rows(r.compact[m], rows).astype(BF16)
        for half in reversed(range(z.flights)):
            spread(way, m, half, reply[half * z.half_rows : (half + 1) * z.half_rows], True)

    def gathered(way, m, half):
        flight = 0 if z.merged else half
        if not z.merged or half == 1:
            settle(REPLY + 100 * way + 10 * m + flight)
        return dot_rows(r.pick[half, m], r.reply_in[way, m, flight].reshape(z.half_rows, model))

    def combine_mirror(way, m):
        r.sums_out[way, m] = gathered(way, m, 1).astype(BF16)
        swap(
            SUMS + 10 * way + m,
            lambda: r.sums_out.at[way, m],
            lambda: r.sums_in.at[way, m],
            lambda: (r.sums_send.at[way, m], r.sums_recv.at[way, m]),
        )

    def combine_end(way, m):
        own = gathered(way, m, 0)
        settle(SUMS + 10 * way + m)
        return own + r.sums_in[way, m].astype(F32)

    greet_back()

    @dec
    def _():
        dispatch(1, 0, r.cotangent)
        settle(0)
        fill_pick(1)
        dispatch_mirror(1, 0, r.cotangent)

    low_lane = jnp.where(iota((1, LANES), 1) < LANES // 2, 1.0, 0.0)
    high_lane = 1.0 - low_lane
    low_bf, high_bf = (low_lane.astype(BF16), high_lane.astype(BF16))
    pairs = model // LANES
    score_scale = (model // HEADS) ** (-0.5)

    def stacked(block):
        return jnp.concatenate([block * low_bf, block * high_bf], axis=0)

    def merged(block):
        return block[:tok] * low_lane + block[tok:] * high_lane

    def attend(queries, keys, values, allowed):
        scores = dot_cols(stacked(queries), keys) * score_scale
        if allowed is not None:
            scores = jnp.where(allowed > 0.5, scores, -1000000000.0)
        top = jnp.max(scores, axis=-1, keepdims=True)
        grown = jnp.exp(scores - top)
        probs = grown / lane_sum(grown)
        return probs, merged(dot(probs.astype(BF16), values))

    def attend_back(queries, keys, values, probs, grad_mixed):
        grad_stack = stacked(grad_mixed)
        grad_probs = dot_cols(grad_stack, values)
        inner = lane_sum(probs * grad_probs)
        grad_scores = (probs * (grad_probs - inner)).astype(BF16)
        grad_queries = merged(dot(grad_scores, keys)) * score_scale
        grad_keys = dot_rows(grad_scores, stacked(queries)) * score_scale
        grad_values = dot_rows(probs.astype(BF16), grad_stack)
        return grad_queries, grad_keys, grad_values

    def cols(index, start=0):
        return pl.ds(pl.multiple_of(start + index * LANES, LANES), LANES)

    def each_pair(run):
        def step(pair, _):
            run(pair)
            return 0

        lax.fori_loop(0, pairs, step, 0, unroll=UNROLL)

    gain_a, gain_c, gain_m = [r.gains[:, i * model : (i + 1) * model] for i in range(3)]

    def enter_experts(m):
        r.normed_m[m] = norm(r.after_cross[m], gain_m).astype(BF16)
        dispatch(0, m, r.normed_m)

    loads[0].wait()
    loads[1].wait()
    for m in range(micro):
        x_in = r.inputs[m].astype(F32)
        normed_a = norm(x_in, gain_a).astype(BF16)
        r.normed_a[m] = normed_a
        r.qkv[m] = dot(normed_a, r.wqkv[...]).astype(BF16)
        causal = jnp.where(iota((tok, tok), 1) <= iota((tok, tok), 0), 1.0, enc_f)
        allowed = when_equal(flipped[:, m : m + 1], seg_rows[m : m + 1]) * causal
        allowed = jnp.concatenate([allowed, allowed], axis=0)
        @each_pair
        def _(pair):
            probs, mixed = attend(
                r.qkv[m, :, cols(pair)],
                r.qkv[m, :, cols(pair, model)],
                r.qkv[m, :, cols(pair, 2 * model)],
                allowed,
            )
            r.probs_self[m, pair] = probs
            r.attn_rows[m, :, cols(pair)] = mixed.astype(BF16)
        after_self = x_in + dot(r.attn_rows[m], r.wout[...])

        @enc
        def _():
            r.after_cross[m] = after_self
            enter_experts(m)

        @dec
        def _():
            r.after_self[m] = after_self

    loads[2].wait()

    def send_memory(m):
        index = m + micro * side[0]
        ship(
            MEMORY + index,
            lambda: r.memory_out.at[m],
            lambda: r.memory.at[m],
            lambda: (r.memory_send.at[index], r.memory_recv.at[index]),
            {"section": 1 - section},
        )

    def wait_memory(m):
        index = m + micro * (1 - side[0])
        owe(MEMORY + index, lambda: (r.memory.at[m], r.memory_recv.at[index]))
        settle(MEMORY + index)

    @enc
    def _():
        settle(0)
        fill_pick(1)

    @dec
    def _():
        for m in range(micro):
            after_self = r.after_self[m]
            normed_c = norm(after_self, gain_c).astype(BF16)
            r.normed_c[m] = normed_c
            r.cross_q[m] = dot(normed_c, r.wcross[:, :model]).astype(BF16)
            wait_memory(m)

            @each_pair
            def _(pair):
                probs, mixed = attend(
                    r.cross_q[m, :, cols(pair)],
                    r.memory[m, :, cols(pair)],
                    r.memory[m, :, cols(pair, model)],
                    None,
                )
                r.probs_cross[m, pair] = probs
                r.cross_rows[m, :, cols(pair)] = mixed.astype(BF16)

            r.after_cross[m] = after_self + dot_cols(r.cross_rows[m], r.wcross[:, model:])
            enter_experts(m)

    for m in range(micro):
        dispatch_mirror(0, m, r.normed_m)

    @dec
    def _():
        for m in range(1, micro):
            dispatch(1, m, r.cotangent)
        for m in range(1, micro):
            dispatch_mirror(1, m, r.cotangent)

    own_task = task_of(me_f)
    partner = lane_sum(when_equal(table_lane, own_task, table[0:1] + table[1:2])) - me_f
    capacity = r.capacity[0].astype(F32)
    place = iota((1, z.all_rows), 1)
    block = whole_part(place, send)
    place_rank = place - block * send
    place_half = whole_part(block, group)
    sender = here_f - (block - place_half * group)
    if z.merged:
        place_half = jnp.minimum(whole_part(place_rank, z.bound), 1.0)
        place_rank = place_rank - place_half * z.bound
    sender = base_f + jnp.where(sender < 0.0, sender + group, sender) + place_half * group
    sender = jnp.where(sender >= z.experts, sender - z.experts, sender)
    teller = me_f - iota((z.experts, 1), 0)
    teller = jnp.where(teller < 0.0, teller + z.experts, teller)
    for m in range(micro):
        told = lane_sum(jnp.where(lane == own_task, r.infos[:, INFO_COUNT + m, :], 0.0))
        count = row_sum(when_equal(teller, sender, told))
        slot = row_sum(jnp.where(teller < sender, told, 0.0)) + place_rank
        slot = jnp.where((place_rank < count) & (slot < capacity), slot, -1.0)
        r.compact[m] = when_equal(iota((slots, 1), 0), slot).astype(BF16)

    first_cross = 0
    first_out = first_cross + z.cross_blocks
    first_qkv = first_out + z.out_blocks
    first_misc = first_qkv + z.qkv_blocks

    def flat(ref, at=slice(None)):
        value = ref[:, :, at]
        return value.reshape(value.shape[0] * value.shape[1], value.shape[2])

    def store_blocks(first, left, right):
        width = 2 * LANES
        left = flat(left)
        for start in range(0, right.shape[-1], width):
            grad = dot_rows(left, flat(right, pl.ds(start, width))).astype(BF16)
            at = (first + start // LANES) * model
            r.dense[at : at + model] = grad[:, :LANES]
            r.dense[at + model : at + 2 * model] = grad[:, LANES:]

    bits = list(range(z.bits))
    lead = min(3, z.bits)
    last_stage = 2 * z.bits
    groups = []
    for group_parts in z.groups:
        made = sum(len(group) for group in groups)
        groups.append([])
        for index, (start, size) in enumerate(group_parts, made):
            turn = index % lead
            even = bits[turn:lead] + bits[:turn] + bits[lead:]
            light = bits[:2] if index % 2 == 0 else bits[:2][::-1]
            orders = (even, light + bits[2:])
            groups[-1].append(SimpleNamespace(index=index, start=start, size=size, orders=orders))

    def stride_of(part, level):
        first, second = [1 << order[level] for order in part.orders]
        return first + section * (second - first)

    def bit_of(part, level):
        return lax.rem(lax.div(me, stride_of(part, level)), 2)

    def rows_of(part, level, offset=0):
        size = part.size >> level
        at = part.start + offset * size
        for upper in range(level):
            at = at + bit_of(part, upper) * (part.size >> (upper + 1))
        return pl.ds(pl.multiple_of(at, 16), size)

    def landing(part, stage):
        return pl.ds(part.start + part.size - (part.size >> stage), part.size >> (stage + 1))

    def transfer(part, stage):
        halving = stage < z.bits
        level = stage if halving else last_stage - 1 - stage
        bit = bit_of(part, level)
        if halving:
            half = part.size >> (stage + 1)
            kept = rows_of(part, stage + 1)
            given = pl.ds(pl.multiple_of(kept.start + (1 - 2 * bit) * half, 16), half)
            source, target = (r.dense.at[given], r.partial.at[landing(part, stage)])
        else:
            source = target = r.total.at[rows_of(part, level + 1)]
        return pltpu.make_async_remote_copy(
            src_ref=source,
            dst_ref=target,
            send_sem=r.sum_send.at[part.index, stage],
            recv_sem=r.sum_recv.at[part.index, stage],
            device_id={"expert": me + (1 - 2 * bit) * stride_of(part, level)},
            device_id_type=MESH,
        )

    def step_group(group, stage):
        for part in groups[group]:
            if stage > 0:
                transfer(part, stage - 1).wait()
            if 0 < stage <= z.bits:
                rows = rows_of(part, stage)
                came = r.partial[landing(part, stage - 1)].astype(F32)
                target = r.total if stage == z.bits else r.dense
                target[rows] = (r.dense[rows].astype(F32) + came).astype(BF16)
            if stage < last_stage:
                transfer(part, stage).start()

    stages = [[0, 0], 0, 0]

    def advance_first(index):
        if stages[0][index] <= last_stage:
            if side[0] == index:
                step_group(0, stages[0][index])
            else:
                on_section(index)(lambda: step_group(0, stages[0][index]))
            stages[0][index] += 1

    def advance(group):
        if group == 0:
            advance_first(0)
            advance_first(1)
        elif stages[group] <= last_stage:
            step_group(group, stages[group])
            stages[group] += 1

    router = r.w_router[...]
    routers = router.shape[0]
    expert_lane = iota((8, routers), 1)
    sign = when_equal(expert_lane, me_f) - when_equal(expert_lane, partner)
    router_step = dot(sign.astype(BF16), router)[0:1]
    tile = 1024

    def each_tile(width, run):
        def step(index, _):
            run(pl.ds(pl.multiple_of(index * tile, tile), tile))
            return 0

        lax.fori_loop(0, width // tile, step, 0)

    def expert_forward(m):
        taken = arrived(0, m).astype(BF16)
        r.taken[m] = taken

        def up_tile(at):
            act, slope = gelu_and_slope(dot(r.taken[m], r.wup[:, at]))
            r.act[m, :, at] = act.astype(BF16)
            r.slope[m, :, at] = slope.astype(BF16)

        each_tile(z.hidden, up_tile)
        gap = lane_sum(taken.astype(F32) * router_step)
        small = jnp.exp(-jnp.abs(gap))
        large = 1.0 / (1.0 + small)
        gate = jnp.where(gap >= 0.0, large, small * large)
        r.gate[m] = gate
        r.gate_slope[m] = small * large * large

        r.expert_out[m] = dot(r.act[m], r.wdown[...]).astype(BF16)
        r.gated[m] = (gate * r.expert_out[m].astype(F32)).astype(BF16)

    def expert_backward(m):
        grad_final = arrived(1, m)
        grad_gate = lane_sum(r.expert_out[m].astype(F32) * grad_final)
        grad_gap = r.gate_slope[m] * grad_gate
        r.grad_gap[m] = grad_gap
        r.grad_out[m] = (r.gate[m] * grad_final).astype(BF16)

        def act_tile(at):
            grad_act = dot_cols(r.grad_out[m], r.wdown[at, :])
            r.grad_hidden[m, :, at] = (grad_act * r.slope[m, :, at].astype(F32)).astype(BF16)

        each_tile(z.hidden, act_tile)

        rounded = dot_cols(r.grad_hidden[m], r.wup[...]).astype(BF16).astype(F32)
        combine(1, m, (rounded + grad_gap * router_step).astype(BF16))

    loads[3].wait()
    loads[4].wait()

    @dec
    def _():
        for m in range(micro):
            expert_forward(m)
            expert_backward(m)
        for m in range(micro):
            combine(0, m, r.gated[m])
            r.grad_state[m] = r.cotangent[m].astype(F32)

    @enc
    def _():
        for m in range(micro):
            expert_forward(m)
            combine(0, m, r.gated[m])
        for m in range(micro):
            combine_mirror(0, m)
        for m in range(micro):
            layer_final = r.after_cross[m] + combine_end(0, m)
            r.layer_final[m] = layer_final
            r.layer_out[m] = layer_final.astype(BF16)
            normed_k = norm(layer_final, gain_c).astype(BF16)
            r.normed_c[m] = normed_k
            r.memory_out[m] = dot(normed_k, r.wcross[...]).astype(BF16)
            send_memory(m)
        gain_grad = jnp.zeros((1, model), F32)
        for m in range(micro):
            wait_memory(m)
            grad_normed = dot_cols(r.memory[m], r.wcross[...])
            grad_state, grad_gain = norm_back(r.layer_final[m], gain_c, grad_normed)
            gain_grad += grad_gain
            grad_final = r.cotangent[m].astype(F32) + grad_state
            r.grad_state[m] = grad_final
            r.grad_rows[m] = grad_final.astype(BF16)
            dispatch(1, m, r.grad_rows)
        for m in range(micro):
            dispatch_mirror(1, m, r.grad_rows)
        r.gain_grads[1:2] = gain_grad
        store_blocks(first_cross, r.normed_c, r.memory)
        for m in range(micro):
            expert_backward(m)
        advance_first(0)

    saves = []

    def save(source, target):
        copy = pltpu.make_async_copy(source, target, r.save_sem.at[len(saves)])
        copy.start()
        saves.append(copy)

    def up_grad(at):
        r.wup[:, at] = dot_rows(flat(r.taken), flat(r.grad_hidden, at)).astype(BF16)

    def down_grad(at):
        r.wdown[at, :] = dot_rows(flat(r.act, at), flat(r.grad_out)).astype(BF16)

    each_tile(z.hidden, up_grad)
    save(r.wup, r.up_grad)
    for m in range(micro):
        combine_mirror(1, m)
    each_tile(z.hidden, down_grad)
    save(r.wdown, r.down_grad)

    gain_grad = jnp.zeros((1, model), F32)
    for m in range(micro):
        grad_state, grad_gain = norm_back(r.after_cross[m], gain_m, combine_end(1, m))
        gain_grad += grad_gain
        r.grad_state[m] += grad_state

        @dec
        def _():
            grad_y = r.grad_state[m].astype(BF16)
            r.grad_cross[m] = grad_y
            r.grad_mix[...] = dot(grad_y, r.wcross[:, model:]).astype(BF16)

            @each_pair
            def _(pair):
                at = cols(pair)
                grad_q, grad_k, grad_v = attend_back(
                    r.cross_q[m, :, at],
                    r.memory[m, :, at],
                    r.memory[m, :, cols(pair, model)],
                    r.probs_cross[m, pair],
                    r.grad_mix[:, at],
                )
                r.grad_cross_q[m, :, at] = grad_q.astype(BF16)
                r.memory_out[m, :, at] = grad_k.astype(BF16)
                r.memory_out[m, :, cols(pair, model)] = grad_v.astype(BF16)
            send_memory(m)

    r.gain_grads[2:3] = gain_grad

    @dec
    def _():
        gain_grad = jnp.zeros((1, model), F32)
        for m in range(micro):
            grad_normed = dot_cols(r.grad_cross_q[m], r.wcross[:, :model])
            grad_state, grad_gain = norm_back(r.after_self[m], gain_c, grad_normed)
            gain_grad += grad_gain
            r.grad_state[m] += grad_state
        r.gain_grads[1:2] = gain_grad

    @dec
    def _():
        store_blocks(first_cross, r.normed_c, r.grad_cross_q)
        store_blocks(first_cross + z.out_blocks, r.grad_cross, r.cross_rows)

    advance_first(1)
    for m in range(micro):
        r.grad_self[m] = r.grad_state[m].astype(BF16)
    store_blocks(first_out, r.attn_rows, r.grad_self)
    advance(1)

    gain_grad = jnp.zeros((1, model), F32)
    for m in range(micro):
        grad_top = r.grad_state[m]
        grad_y = r.grad_self[m]
        r.grad_mix[...] = dot_cols(grad_y, r.wout[...]).astype(BF16)

        @each_pair
        def _(pair):
            grads = attend_back(
                r.qkv[m, :, cols(pair)],
                r.qkv[m, :, cols(pair, model)],
                r.qkv[m, :, cols(pair, 2 * model)],
                r.probs_self[m, pair],
                r.grad_mix[:, cols(pair)],
            )
            for third, grad in enumerate(grads):
                r.grad_qkv[m, :, cols(pair, third * model)] = grad.astype(BF16)
        grad_normed = dot_cols(r.grad_qkv[m], r.wqkv[...])
        grad_state, grad_gain = norm_back(r.inputs[m].astype(F32), gain_a, grad_normed)
        gain_grad += grad_gain
        r.inputs_grad[m] = grad_top + grad_state
    r.gain_grads[0:1] = gain_grad
    r.gain_grads[3:8] = jnp.zeros((5, model), F32)

    store_blocks(first_qkv, r.normed_a, r.grad_qkv)
    misc_row = iota((1, z.misc), 1)
    misc_sign = when_equal(misc_row, me_f) - when_equal(misc_row, partner)
    misc = jnp.zeros((z.misc, model), F32)
    for m in range(micro):
        steps = r.grad_gap[m] * misc_sign
        top = steps.astype(BF16)
        rest = (steps - top.astype(F32)).astype(BF16)
        misc += dot_rows(top, r.taken[m]) + dot_rows(rest, r.taken[m])
    place_gain = when_equal(iota((8, z.misc), 1), iota((8, z.misc), 0) + routers)
    misc += dot_rows(place_gain.astype(BF16), r.gain_grads[...].astype(BF16))
    misc_rows = [
        pl.ds(first_misc * model + index * z.misc, z.misc) for index in range(model // LANES)
    ]
    for index, rows in enumerate(misc_rows):
        r.dense[rows] = misc[:, index * LANES : (index + 1) * LANES].astype(BF16)
    used = z.blocks * model
    if used < z.dense_rows:
        r.dense[used:] = jnp.zeros((z.dense_rows - used, LANES), BF16)
    advance(2)
    advance(0)
    advance(1)

    @dec
    def _():
        for m in range(micro):
            combine_mirror(0, m)
        for m in range(micro):
            r.layer_out[m] = (r.after_cross[m] + combine_end(0, m)).astype(BF16)

    def save_blocks(target, first, count):
        for index in range(count):
            rows = pl.ds((first + index) * model, model)
            save(r.total.at[rows], target.at[:, pl.ds(index * LANES, LANES)])

    while stages[2] <= last_stage:
        if stages[0][1] <= last_stage:
            advance(0)
            if stages[0][1] > last_stage:
                save_blocks(r.cross_grad, first_cross, z.cross_blocks)
        if stages[1] <= last_stage:
            advance(1)
            if stages[1] > last_stage:
                save_blocks(r.out_grad, first_out, z.out_blocks)
        advance(2)
    save_blocks(r.qkv_grad, first_qkv, z.qkv_blocks)

    for index, rows in enumerate(misc_rows):
        sums = r.total[rows].astype(F32)
        r.router_grad[:, index * LANES : (index + 1) * LANES] = sums[:routers]
        for row in range(3):
            at = row * model + index * LANES
            r.gains_grad[:, at : at + LANES] = sums[routers + row : routers + row + 1]
    for copy in saves:
        copy.wait()

    settle_all()


def vmem_bytes(buffers):
    total = 0
    for buffer in buffers:
        if buffer.memory_space == pltpu.VMEM:
            *lead, rows, lanes = buffer.shape
            size = math.prod(lead) * round_up(rows, 8) * round_up(lanes, LANES)
            total += size * jnp.dtype(buffer.dtype).itemsize
    return min(total + 5 * 1024 * 1024, 62 * 1024 * 1024)


def run_kernel(z, arrays):
    micro, tok, model, hidden = (z.micro, z.tok, z.model, z.hidden)
    vmem = pl.BlockSpec(memory_space=pltpu.VMEM)
    hbm = pl.BlockSpec(memory_space=pl.ANY)
    inputs = dict(
        segments=(arrays.segments, vmem),
        tasks=(arrays.tasks, vmem),
        table=(arrays.table, vmem),
        capacity=(arrays.capacity, pl.BlockSpec(memory_space=pltpu.SMEM)),
        inputs=(arrays.inputs, vmem),
        cotangent=(arrays.cotangent, vmem),
        gains=(arrays.gains, vmem),
        w_router=(arrays.w_router, vmem),
        w_qkv=(arrays.w_qkv, hbm),
        w_out=(arrays.w_out, hbm),
        w_cross=(arrays.w_cross, hbm),
        w_up=(arrays.w_up, hbm),
        w_down=(arrays.w_down, hbm),
    )
    rows = (micro, tok, model)
    slot_rows = (micro, z.slots, model)
    slot_hidden = (micro, z.slots, hidden)
    outputs = dict(
        layer_out=(rows, BF16, vmem),
        inputs_grad=(rows, F32, vmem),
        gains_grad=((1, 3 * model), F32, vmem),
        router_grad=(arrays.w_router.shape, F32, vmem),
        qkv_grad=(arrays.w_qkv.shape, BF16, hbm),
        out_grad=(arrays.w_out.shape, BF16, hbm),
        cross_grad=(arrays.w_cross.shape, BF16, hbm),
        up_grad=(arrays.w_up.shape, BF16, hbm),
        down_grad=(arrays.w_down.shape, BF16, hbm),
    )
    blocks = (2, micro, z.flights, z.group, z.send, model)
    pairs = model // LANES
    dma = pltpu.SemaphoreType.DMA
    scratch = dict(
        wqkv=pltpu.VMEM(arrays.w_qkv.shape, BF16),
        wout=pltpu.VMEM(arrays.w_out.shape, BF16),
        wcross=pltpu.VMEM(arrays.w_cross.shape, BF16),
        wup=pltpu.VMEM(arrays.w_up.shape, BF16),
        wdown=pltpu.VMEM(arrays.w_down.shape, BF16),
        infos=pltpu.VMEM((z.experts, 8, LANES), F32),
        normed_a=pltpu.VMEM(rows, BF16),
        qkv=pltpu.VMEM((micro, tok, 3 * model), BF16),
        probs_self=pltpu.VMEM((micro, pairs, 2 * tok, tok), F32),
        attn_rows=pltpu.VMEM(rows, BF16),
        after_self=pltpu.VMEM(rows, F32),
        normed_c=pltpu.VMEM(rows, BF16),
        cross_q=pltpu.VMEM(rows, BF16),
        probs_cross=pltpu.VMEM((micro, pairs, 2 * tok, tok), F32),
        cross_rows=pltpu.VMEM(rows, BF16),
        memory_out=pltpu.VMEM((micro, tok, 2 * model), BF16),
        memory=pltpu.VMEM((micro, tok, 2 * model), BF16),
        after_cross=pltpu.VMEM(rows, F32),
        normed_m=pltpu.VMEM(rows, BF16),
        layer_final=pltpu.VMEM(rows, F32),
        grad_state=pltpu.VMEM(rows, F32),
        grad_rows=pltpu.VMEM(rows, BF16),
        grad_cross=pltpu.VMEM(rows, BF16),
        grad_cross_q=pltpu.VMEM(rows, BF16),
        grad_self=pltpu.VMEM(rows, BF16),
        grad_mix=pltpu.VMEM((tok, model), BF16),
        grad_qkv=pltpu.VMEM((micro, tok, 3 * model), BF16),
        gain_grads=pltpu.VMEM((8, model), F32),
        pick=pltpu.VMEM((z.halves, micro, z.half_rows, tok), BF16),
        compact=pltpu.VMEM((micro, z.slots, z.all_rows), BF16),
        rows_out=pltpu.VMEM(blocks, BF16),
        rows_in=pltpu.VMEM(blocks, BF16),
        reply_out=pltpu.VMEM(blocks, BF16),
        reply_in=pltpu.VMEM(blocks, BF16),
        mirror_rows=pltpu.VMEM((2,) + rows, BF16),
        sums_out=pltpu.VMEM((2,) + rows, BF16),
        sums_in=pltpu.VMEM((2,) + rows, BF16),
        taken=pltpu.VMEM(slot_rows, BF16),
        slope=pltpu.VMEM(slot_hidden, BF16),
        act=pltpu.VMEM(slot_hidden, BF16),
        expert_out=pltpu.VMEM(slot_rows, BF16),
        gated=pltpu.VMEM(slot_rows, BF16),
        gate=pltpu.VMEM((micro, z.slots, 1), F32),
        gate_slope=pltpu.VMEM((micro, z.slots, 1), F32),
        grad_gap=pltpu.VMEM((micro, z.slots, 1), F32),
        grad_out=pltpu.VMEM(slot_rows, BF16),
        grad_hidden=pltpu.VMEM(slot_hidden, BF16),
        dense=pltpu.VMEM((z.dense_rows, LANES), BF16),
        total=pltpu.VMEM((z.dense_rows, LANES), BF16),
        partial=pltpu.VMEM((z.dense_rows, LANES), BF16),
        load_sem=dma((5,)),
        save_sem=dma((2 + z.blocks - z.misc_blocks,)),
        info_send=dma(()),
        info_recv=dma(()),
        rows_send=dma((2, micro, z.flights)),
        rows_recv=dma((2, micro, z.flights)),
        reply_send=dma((2, micro, z.flights)),
        reply_recv=dma((2, micro, z.flights)),
        mirror_send=dma((2, micro)),
        mirror_recv=dma((2, micro)),
        sums_send=dma((2, micro)),
        sums_recv=dma((2, micro)),
        memory_send=dma((2 * micro,)),
        memory_recv=dma((2 * micro,)),
        sum_send=dma((z.parts, 2 * z.bits)),
        sum_recv=dma((z.parts, 2 * z.bits)),
    )
    names = [*inputs, *outputs, *scratch]

    def body(*refs):
        kernel_body(z, names, *refs)

    return pl.pallas_call(
        body,
        name="layer_step",
        out_shape=[jax.ShapeDtypeStruct(shape, dtype) for shape, dtype, _ in outputs.values()],
        in_specs=[spec for _, spec in inputs.values()],
        out_specs=[spec for _, _, spec in outputs.values()],
        scratch_shapes=list(scratch.values()),
        compiler_params=pltpu.CompilerParams(
            collective_id=0, has_side_effects=True, vmem_limit_bytes=vmem_bytes(scratch.values())
        ),
    )(*[value for value, _ in inputs.values()])


def widen_body(count, *refs):
    total = (len(refs) - 2) // 4
    sources, targets, came, made = [refs[i * total : (i + 1) * total] for i in range(4)]
    come_sem, go_sem = refs[4 * total :]
    loads = [pltpu.make_async_copy(sources[i], came[i], come_sem.at[i]) for i in range(total)]
    for copy in loads:
        copy.start()
    for i in range(total):
        loads[i].wait()
        if i >= count:
            pltpu.make_async_copy(came[i], targets[i], go_sem.at[i]).start()
            continue
        rows, lanes = came[i].shape
        step_rows = 1 << (min(rows, 128 * 1024 // lanes).bit_length() - 1)

        def step(index, _):
            at = pl.ds(pl.multiple_of(index * step_rows, step_rows), step_rows)
            made[i][at] = came[i][at].astype(F32)
            pltpu.make_async_copy(made[i].at[at], targets[i].at[at], go_sem.at[i]).start()
            return 0

        lax.fori_loop(0, rows // step_rows, step, 0)
    for i in range(total):
        left = made[i] if i < count else came[i]
        pltpu.make_async_copy(left, targets[i], go_sem.at[i]).wait()


def widen(narrow, passed):
    values = [*narrow, *passed]
    count = len(narrow)
    types = [F32] * count + [value.dtype for value in passed]
    hbm = pl.BlockSpec(memory_space=pltpu.HBM)
    dma = pltpu.SemaphoreType.DMA((len(values),))
    blank = pltpu.VMEM((8, LANES), F32)
    return pl.pallas_call(
        lambda *refs: widen_body(count, *refs),
        name="widen",
        out_shape=[jax.ShapeDtypeStruct(v.shape, t) for v, t in zip(values, types)],
        in_specs=[hbm] * len(values),
        out_specs=[hbm] * len(values),
        scratch_shapes=[pltpu.VMEM(value.shape, value.dtype) for value in values]
        + [pltpu.VMEM(value.shape, F32) for value in narrow]
        + [blank] * len(passed)
        + [dma, dma],
        compiler_params=pltpu.CompilerParams(vmem_limit_bytes=62 * 1024 * 1024),
    )(*values)


def shards(
    inputs,
    cotangent,
    segments,
    tasks,
    table,
    capacity,
    gains,
    w_qkv,
    w_out,
    w_cross,
    w_router,
    w_up,
    w_down,
):
    experts = lax.axis_size("expert")
    z = Sizes(inputs, w_qkv, w_cross, w_router, w_up, table, experts)
    model = z.model
    arrays = SimpleNamespace(
        segments=segments[0],
        tasks=tasks[0, :, :, 0],
        table=table[0].T,
        capacity=capacity,
        inputs=inputs[0],
        cotangent=cotangent[0],
        gains=gains.reshape(1, 3 * model),
        w_router=w_router[0].T,
        w_qkv=w_qkv[0],
        w_out=w_out[0],
        w_cross=w_cross[0],
        w_up=w_up[0, 0],
        w_down=w_down[0, 0],
    )
    *passed, qkv_grad, out_grad, cross_grad, up_grad, down_grad = run_kernel(z, arrays)
    narrow = (up_grad, down_grad, qkv_grad, cross_grad, out_grad)
    up_grad, down_grad, qkv_grad, cross_grad, out_grad, *passed = widen(narrow, passed)
    out, inputs_grad, gains_grad, router_grad = passed
    return (
        out[None],
        inputs_grad[None],
        gains_grad.reshape(1, 3, model),
        qkv_grad[None],
        out_grad[None],
        cross_grad[None],
        router_grad.T[None],
        up_grad[None, None],
        down_grad[None, None],
    )


def solution(mesh):
    in_specs = (
        P("section", None, "expert", None),
        P("section", None, "expert", None),
        P("section", None, "expert"),
        P("section", None, "expert", None),
        P("section", None, None),
        P("section"),
        P("section", None, None),
        P("section", None, None),
        P("section", None, None),
        P("section", None, None),
        P("section", None, None),
        P("section", "expert", None, None),
        P("section", "expert", None, None),
    )
    out_specs = (
        P("section", None, "expert", None),
        P("section", None, "expert", None),
        P("section", None, None),
        P("section", None, None),
        P("section", None, None),
        P("section", None, None),
        P("section", None, None),
        P("section", "expert", None, None),
        P("section", "expert", None, None),
    )
    return jax.shard_map(shards, mesh=mesh, in_specs=in_specs, out_specs=out_specs, check_vma=False)
```

profile of v0, /device:TPU:0, one launch (start us, length us, event | category | flops | bytes accessed | tf_op | source)
XLA Modules:
  0.0 183.2 jit_solution(484650587204961168)
XLA Ops:
  1.3 174.1 %layer_step.1 = (bf16[2,128,512]{2,1,0:T(8,128)(2,1)}, f32[2,128,512]{2,1,0:T(8,128)}, f32[1,1536]{1,0:T(1,128)}, f32[16,512]{1,0:T(8,128)}, bf16[512,1536]{1,0:...) custom-call(s32[2,128]{1,0:T(2,128)} %bitcast.36, ...), custom_call_target="tpu_custom_call" | custom-call | tf_op jit(solution)/shard_map/layer_step/pallas_call | solution.py:995
  175.4 7.5 %widen.1 = (f32[512,2048]{1,0:T(8,128)}, f32[2048,512]{1,0:T(8,128)}, f32[512,1536]{1,0:T(8,128)}, f32[512,1024]{1,0:T(8,128)}, f32[512,512]{1,0:T(8,128)}, /*in...) custom-call(bf16[512,2048]{1,0:T(8,128)(2,1)} %get-tuple-element.27.refs_0_, ...), custom_call_target="tpu_custom_call" | custom-call | tf_op jit(solution)/shard_map/widen/pallas_call | solution.py:1042
where the time goes:
time: 183 us
  Pallas kernels  182 us (99%)
    pallas_call x1, Pallas kernels, run_kernel(): pl.pallas_call(body, name='layer_step', out_shape=[jax.ShapeDtypeStruct(s...  174 us
    pallas_call x1, Pallas kernels, widen(): pl.pallas_call(lambda *refs: widen_body(count, *refs), name='widen', out_...  7.53 us

commit v1 on v0

--- a/solution.py
+++ b/solution.py
@@ -1087,8 +1087,8 @@
         w_down=w_down[0, 0],
     )
     *passed, qkv_grad, out_grad, cross_grad, up_grad, down_grad = run_kernel(z, arrays)
-    narrow = (up_grad, down_grad, qkv_grad, cross_grad, out_grad)
-    up_grad, down_grad, qkv_grad, cross_grad, out_grad, *passed = widen(narrow, passed)
+    narrow = (out_grad, cross_grad, qkv_grad, up_grad, down_grad)
+    out_grad, cross_grad, qkv_grad, up_grad, down_grad, *passed = widen(narrow, passed)
     out, inputs_grad, gains_grad, router_grad = passed
     return (
         out[None],

time: 183 us -> 184 us (level)
  no operation moved by 1% of the time
where the time goes in v1:
time: 184 us
  Pallas kernels  182 us (99%)
    pallas_call x1, Pallas kernels, run_kernel(): pl.pallas_call(body, name='layer_step', out_shape=[jax.ShapeDtypeStruct(s...  174 us
    pallas_call x1, Pallas kernels, widen(): pl.pallas_call(lambda *refs: widen_body(count, *refs), name='widen', out_...  8.13 us

profile of v1, /device:TPU:0, one launch (start us, length us, event | category | flops | bytes accessed | tf_op | source)
XLA Modules:
  0.0 183.8 jit_solution(8859864209930167566)
XLA Ops:
  1.3 174.1 %layer_step.1 = (bf16[2,128,512]{2,1,0:T(8,128)(2,1)}, f32[2,128,512]{2,1,0:T(8,128)}, f32[1,1536]{1,0:T(1,128)}, f32[16,512]{1,0:T(8,128)}, bf16[512,1536]{1,0:...) custom-call(s32[2,128]{1,0:T(2,128)} %bitcast.36, ...), custom_call_target="tpu_custom_call" | custom-call | tf_op jit(solution)/shard_map/layer_step/pallas_call | solution.py:995
  175.4 8.1 %widen.1 = (f32[512,512]{1,0:T(8,128)}, f32[512,1024]{1,0:T(8,128)}, f32[512,1536]{1,0:T(8,128)}, f32[512,2048]{1,0:T(8,128)}, f32[2048,512]{1,0:T(8,128)}, /*in...) custom-call(bf16[512,512]{1,0:T(8,128)(2,1)} %get-tuple-element.27.refs_0_, ...), custom_call_target="tpu_custom_call" | custom-call | tf_op jit(solution)/shard_map/widen/pallas_call | solution.py:1042
